TPU v7x, 256 devices: a whole 4x4x8 slice. The times are simulated.
256 devices in a mesh: wide: 64 (over y, z, core), grp: 4 (over x).
Axes of the slice: x: 4, y: 4, z: 8, core: 2. Of those that a mesh axis runs over, the one named last changes fastest.
Arguments:
- slab: float32 [512, 4, 128, 128], P(None, 'grp', 'wide'), may hold values from -400 to 400
- hblocks: float32 [4, 128, 5, 128, 128], P('grp', 'wide'), may hold values from -0.25 to 0.25
- blist: int32 [4, 128, 5], P('grp', 'wide'), may hold values from 0 to 8, as said below
- rotation: float32 [64, 8, 8], replicated, may hold values from -2 to 2
Outputs:
- rotated: float32 [512, 4, 128, 128], P('wide', 'grp')
Inputs may be any that keep to these rules, and one draw needn't show every extreme that they name: `blist`: entry 0 of every row block's list is 4 (the block itself); the other entries are distinct codes other than 4.
All inputs are finite; a program needn't handle non-finite values.
Results may differ from a plain program's by a relative error of at most 0.00012.
Values sent between devices are 32-bit elements; how exact they have to be, the bound alone decides.
A program may use at most 64 MiB of HBM per device.

v0:
```python
import jax
import jax.numpy as jnp
from jax import lax
from jax.sharding import PartitionSpec as P

VEC = 8
DEG = 4


def with_halo(block, sides, width):
    for axis, dim in sides:
        count = lax.axis_size(axis)
        forward = [(i, i + 1) for i in range(count - 1)]
        backward = [(target, source) for source, target in forward]
        low = lax.ppermute(
            lax.slice_in_dim(block, block.shape[dim] - width, None, axis=dim), axis, forward
        )
        high = lax.ppermute(lax.slice_in_dim(block, 0, width, axis=dim), axis, backward)
        block = jnp.concatenate([low, block, high], axis=dim)
    return block


def combine_slots(extended, hblocks, blist):
    states = extended.shape[0]
    grid_rows, blocks_here, slot_count, block_nodes = (
        hblocks.shape[0],
        hblocks.shape[1],
        hblocks.shape[2],
        hblocks.shape[3],
    )
    flat_ext = extended.reshape(states, (grid_rows + 2) * (blocks_here + 2), block_nodes)
    row_index = jnp.arange(grid_rows, dtype=jnp.int32)[:, None]
    col_index = jnp.arange(blocks_here, dtype=jnp.int32)[None, :]
    summed = jnp.zeros((states, grid_rows * blocks_here, block_nodes), jnp.float32)
    for slot_index in range(slot_count):
        block_code = blist[:, :, slot_index]
        position = (
            (row_index + block_code // 3) * (blocks_here + 2) + col_index + block_code % 3
        ).reshape(-1)
        picked = jnp.take(flat_ext, position, axis=1)
        weights_here = hblocks[:, :, slot_index].reshape(
            grid_rows * blocks_here, block_nodes, block_nodes
        )
        summed = summed + jnp.einsum(
            "rij,srj->sri", weights_here, picked, precision=lax.Precision.HIGHEST
        )
    return summed.reshape(states, grid_rows, blocks_here, block_nodes)


def apply_rows(field_in, hblocks, blist):
    extended = with_halo(field_in, (("wide", 2), ("grp", 1)), 1)
    return combine_slots(extended, hblocks, blist)


def chebyshev(start, operator_fn):
    previous = start
    current = operator_fn(start)
    for degree_step in range(DEG - 1):
        following = 2.0 * operator_fn(current) - previous
        previous, current = (current, following)
    return current


def mixing(gram_mat, rotation):
    lower = jnp.linalg.cholesky(gram_mat)
    return lax.linalg.triangular_solve(
        lower, jnp.swapaxes(rotation, -1, -2), left_side=False, lower=True
    )


def body(slab, hblocks, blist, rotation):
    current = chebyshev(slab, lambda field_in: apply_rows(field_in, hblocks, blist))
    node_count = (
        slab.shape[1] * slab.shape[2] * slab.shape[3] * lax.axis_size("wide") * lax.axis_size("grp")
    )
    state_blocks = current.reshape(rotation.shape[0], VEC, -1)
    partial_gram = jnp.einsum(
        "bam,bcm->bac", state_blocks, state_blocks, precision=lax.Precision.HIGHEST
    )
    gram_mat = lax.psum(partial_gram, ("wide", "grp")) / node_count
    mixer = mixing(gram_mat, rotation)
    mixed_rows = jnp.einsum("bad,bdm->bam", mixer, state_blocks, precision=lax.Precision.HIGHEST)
    rotated = lax.all_to_all(
        mixed_rows.reshape(current.shape), "wide", split_axis=0, concat_axis=2, tiled=True
    )
    return rotated


def solution(mesh):
    in_specs = (
        P(None, "grp", "wide", None),
        P("grp", "wide", None, None, None),
        P("grp", "wide", None),
        P(),
    )
    out_specs = P("wide", "grp", None, None)
    return jax.shard_map(body, mesh=mesh, in_specs=in_specs, out_specs=out_specs, check_vma=False)
```

profile of v0, /device:TPU:1, one launch (start us, length us, event | category | flops | bytes accessed | tf_op | source)
XLA Modules:
  0.0 395.7 jit_solution(18353527175832131404)
XLA Ops:
  1.7 4.9 %collective-permute-start = (f32[512,1,1,128]{3,0,2,1:T(8,128)S(1)}, f32[512,1,1,128]{3,0,2,1:T(8,128)S(1)}, u32[]{:S(2)}, u32[]{:S(2)}) collective-permute-start(f32[512,1,1,128]{3,0,2,1:T(8,128)S(1)} %copy.79), channel_id=1, source_target_pairs={{0,4},{4,8},{8,12},{12,16},{16,20},{20,24},{24,28},{28,32},{32,36}... | collective-permute-start | bytes 786440 | tf_op jit(solution)/shard_map/ppermute | solution.py:15
  14.4 3.2 collective-permute-start.2
  19.1 17.6 %collective-permute-done.2 = f32[512,1,4,128]{3,0,2,1:T(8,128)S(1)} collective-permute-done((f32[512,1,4,128]{3,0,2,1:T(8,128)S(1)}, f32[512,1,4,128]{3,0,2,1:T(8,128)S(1)}, u32[]{:S(2)}, u32[]{:S(2)}) %collective-permute-start.2) | collective-permute-done | bytes 1048608 | tf_op jit(solution)/shard_map/ppermute | solution.py:15
  36.7 4.2 %collective-permute-done.3 = f32[512,1,4,128]{3,0,2,1:T(8,128)S(1)} collective-permute-done((f32[512,1,4,128]{3,0,2,1:T(8,128)S(1)}, f32[512,1,4,128]{3,0,2,1:T(8,128)S(1)}, u32[]{:S(2)}, u32[]{:S(2)}) %collective-permute-start.3) | collective-permute-done | bytes 1048608 | tf_op jit(solution)/shard_map/ppermute | solution.py:18
  54.5 5.7 %collective-permute-start.4 = (f32[512,1,1,128]{3,0,2,1:T(8,128)S(1)}, f32[512,1,1,128]{3,0,2,1:T(8,128)S(1)}, u32[]{:S(2)}, u32[]{:S(2)}) collective-permute-start(f32[512,1,1,128]{3,0,2,1:T(8,128)S(1)} %get-tuple-element.35), channel_id=1, source_target_pairs={{0,4},{4,8},{8,12},{12,16},{16,20},{20,24},{24,28},{28,32},{32,36}... | collective-permute-start | bytes 786440 | tf_op jit(solution)/shard_map/ppermute | solution.py:15
  63.6 4.4 %collective-permute-done.5 = f32[512,1,1,128]{3,0,2,1:T(8,128)S(1)} collective-permute-done((f32[512,1,1,128]{3,0,2,1:T(8,128)S(1)}, f32[512,1,1,128]{3,0,2,1:T(8,128)S(1)}, u32[]{:S(2)}, u32[]{:S(2)}) %collective-permute-start.5) | collective-permute-done | bytes 262176 | tf_op jit(solution)/shard_map/ppermute | solution.py:18
  72.5 17.8 %collective-permute-done.6 = f32[512,1,4,128]{3,0,2,1:T(8,128)S(1)} collective-permute-done((f32[512,1,4,128]{3,0,2,1:T(8,128)S(1)}, f32[512,1,4,128]{3,0,2,1:T(8,128)S(1)}, u32[]{:S(2)}, u32[]{:S(2)}) %collective-permute-start.6) | collective-permute-done | bytes 1048608 | tf_op jit(solution)/shard_map/ppermute | solution.py:15
  90.3 4.2 %collective-permute-done.7 = f32[512,1,4,128]{3,0,2,1:T(8,128)S(1)} collective-permute-done((f32[512,1,4,128]{3,0,2,1:T(8,128)S(1)}, f32[512,1,4,128]{3,0,2,1:T(8,128)S(1)}, u32[]{:S(2)}, u32[]{:S(2)}) %collective-permute-start.7) | collective-permute-done | bytes 1048608 | tf_op jit(solution)/shard_map/ppermute | solution.py:18
  96.3 3.3 gather_fusion.5
  114.0 5.7 %collective-permute-start.8 = (f32[512,1,1,128]{3,0,2,1:T(8,128)S(1)}, f32[512,1,1,128]{3,0,2,1:T(8,128)S(1)}, u32[]{:S(2)}, u32[]{:S(2)}) collective-permute-start(f32[512,1,1,128]{3,0,2,1:T(8,128)S(1)} %get-tuple-element.33), channel_id=1, source_target_pairs={{0,4},{4,8},{8,12},{12,16},{16,20},{20,24},{24,28},{28,32},{32,36}... | collective-permute-start | bytes 786440 | tf_op jit(solution)/shard_map/ppermute | solution.py:15
  123.0 4.4 %collective-permute-done.9 = f32[512,1,1,128]{3,0,2,1:T(8,128)S(1)} collective-permute-done((f32[512,1,1,128]{3,0,2,1:T(8,128)S(1)}, f32[512,1,1,128]{3,0,2,1:T(8,128)S(1)}, u32[]{:S(2)}, u32[]{:S(2)}) %collective-permute-start.9) | collective-permute-done | bytes 262176 | tf_op jit(solution)/shard_map/ppermute | solution.py:18
  131.8 17.6 %collective-permute-done.10 = f32[512,1,4,128]{3,0,2,1:T(8,128)S(1)} collective-permute-done((f32[512,1,4,128]{3,0,2,1:T(8,128)S(1)}, f32[512,1,4,128]{3,0,2,1:T(8,128)S(1)}, u32[]{:S(2)}, u32[]{:S(2)}) %collective-permute-start.10) | collective-permute-done | bytes 1048608 | tf_op jit(solution)/shard_map/ppermute | solution.py:15
  149.4 4.2 %collective-permute-done.11 = f32[512,1,4,128]{3,0,2,1:T(8,128)S(1)} collective-permute-done((f32[512,1,4,128]{3,0,2,1:T(8,128)S(1)}, f32[512,1,4,128]{3,0,2,1:T(8,128)S(1)}, u32[]{:S(2)}, u32[]{:S(2)}) %collective-permute-start.11) | collective-permute-done | bytes 1048608 | tf_op jit(solution)/shard_map/ppermute | solution.py:18
  155.5 3.3 gather_fusion.10
  158.8 3.3 gather_fusion.11
  174.9 4.8 %collective-permute-start.12 = (f32[512,1,1,128]{3,0,2,1:T(8,128)S(1)}, f32[512,1,1,128]{3,0,2,1:T(8,128)S(1)}, u32[]{:S(2)}, u32[]{:S(2)}) collective-permute-start(f32[512,1,1,128]{3,0,2,1:T(8,128)S(1)} %get-tuple-element.31), channel_id=1, source_target_pairs={{0,4},{4,8},{8,12},{12,16},{16,20},{20,24},{24,28},{28,32},{32,36}... | collective-permute-start | bytes 786440 | tf_op jit(solution)/shard_map/ppermute | solution.py:15
  183.0 4.4 %collective-permute-done.13 = f32[512,1,1,128]{3,0,2,1:T(8,128)S(1)} collective-permute-done((f32[512,1,1,128]{3,0,2,1:T(8,128)S(1)}, f32[512,1,1,128]{3,0,2,1:T(8,128)S(1)}, u32[]{:S(2)}, u32[]{:S(2)}) %collective-permute-start.13) | collective-permute-done | bytes 262176 | tf_op jit(solution)/shard_map/ppermute | solution.py:18
  193.4 14.5 %collective-permute-done.14 = f32[512,1,4,128]{3,0,2,1:T(8,128)} collective-permute-done((f32[512,1,4,128]{3,0,2,1:T(8,128)S(1)}, f32[512,1,4,128]{3,0,2,1:T(8,128)}, u32[]{:S(2)}, u32[]{:S(2)}) %collective-permute-start.14) | collective-permute-done | bytes 1048608 | tf_op jit(solution)/shard_map/ppermute | solution.py:15
  207.9 5.2 %collective-permute-done.15 = f32[512,1,4,128]{3,0,2,1:T(8,128)} collective-permute-done((f32[512,1,4,128]{3,0,2,1:T(8,128)S(1)}, f32[512,1,4,128]{3,0,2,1:T(8,128)}, u32[]{:S(2)}, u32[]{:S(2)}) %collective-permute-start.15) | collective-permute-done | bytes 1048608 | tf_op jit(solution)/shard_map/ppermute | solution.py:18
  213.1 3.4 pad_maximum_fusion.3
  216.5 3.4 gather_fusion.15
  236.2 82.8 %psum.7 = f32[64,8,8]{0,1,2:T(8,128)S(1)} all-reduce(f32[64,8,8]{0,1,2:T(8,128)S(1)} %copy.60), channel_id=1, replica_groups=mesh['wide'=64,'grp'=4] {'wide','grp'}, use_global_device_ids=true, to_apply=%region_0.2 | all-reduce | flops 4096 | bytes 32768 | tf_op jit(solution)/shard_map/psum | solution.py:80
  319.2 47.0 %custom-call.7 = f32[64,8,8]{2,1,0:T(8,128)S(1)} custom-call(f32[64,8,8]{2,1,0:T(8,128)S(1)} %broadcast_multiply_fusion), custom_call_target="Cholesky" | custom-call | tf_op jit(solution)/shard_map/jit(cholesky)/cholesky | solution.py:65
  368.9 25.8 %all_to_all.18 = f32[512,1,2,128]{3,2,1,0:T(2,128)S(1)} all-to-all(f32[512,1,2,128]{3,2,1,0:T(2,128)S(1)} %bitcast.184), channel_id=1, replica_groups=mesh['wide'=64,'grp'=4] {'wide'}, dimensions={0} | all-to-all | bytes 1048576 | tf_op jit(solution)/shard_map/all_to_all | solution.py:83
  (124 shorter events, 100.0 us)
Async XLA Ops:
  1.7 9.2 %collective-permute-start = (f32[512,1,1,128]{3,0,2,1:T(8,128)S(1)}, f32[512,1,1,128]{3,0,2,1:T(8,128)S(1)}, u32[]{:S(2)}, u32[]{:S(2)}) collective-permute-start(f32[512,1,1,128]{3,0,2,1:T(8,128)S(1)} %copy.79), channel_id=1, source_target_pairs={{0,4},{4,8},{8,12},{12,16},{16,20},{20,24},{24,28},{28,32},{32,36}... | collective-permute-start | bytes 786440 | tf_op jit(solution)/shard_map/ppermute | solution.py:15
  6.7 7.7 %collective-permute-start.1 = (f32[512,1,1,128]{3,0,2,1:T(8,128)S(1)}, f32[512,1,1,128]{3,0,2,1:T(8,128)S(1)}, u32[]{:S(2)}, u32[]{:S(2)}) collective-permute-start(f32[512,1,1,128]{3,0,2,1:T(8,128)S(1)} %copy.80), channel_id=1, source_target_pairs={{4,0},{8,4},{12,8},{16,12},{20,16},{24,20},{28,24},{32,28},{36,32}... | collective-permute-start | bytes 786440 | tf_op jit(solution)/shard_map/ppermute | solution.py:18
  14.4 22.3 %collective-permute-start.2 = (f32[512,1,4,128]{3,0,2,1:T(8,128)S(1)}, f32[512,1,4,128]{3,0,2,1:T(8,128)S(1)}, u32[]{:S(2)}, u32[]{:S(2)}) collective-permute-start(f32[512,1,4,128]{3,0,2,1:T(8,128)S(1)} %constant_dynamic-update-slice_fusion), channel_id=1, source_target_pairs={{0,1},{1,2},{2,3},{4,5},{5,6},{6,7},{8,9},{9,10},{10,11},{12,13},{... | collective-permute-start | bytes 3145736 | tf_op jit(solution)/shard_map/ppermute | solution.py:15
  17.6 23.3 %collective-permute-start.3 = (f32[512,1,4,128]{3,0,2,1:T(8,128)S(1)}, f32[512,1,4,128]{3,0,2,1:T(8,128)S(1)}, u32[]{:S(2)}, u32[]{:S(2)}) collective-permute-start(f32[512,1,4,128]{3,0,2,1:T(8,128)S(1)} %constant_dynamic-update-slice_fusion), channel_id=1, source_target_pairs={{1,0},{2,1},{3,2},{5,4},{6,5},{7,6},{9,8},{10,9},{11,10},{13,12},{... | collective-permute-start | bytes 3145736 | tf_op jit(solution)/shard_map/ppermute | solution.py:18
  18.9 150.6 %copy-start.5 = (pred[2]{0:T(512)(128)(4,1)}, pred[2]{0:T(512)(128)(4,1)S(1)}, u32[]{:S(2)}) copy-start(pred[2]{0:T(512)(128)(4,1)S(1)} %get-tuple-element.29) | copy-start | bytes 10
  18.9 136.6 %copy-start.6 = (s32[1024]{0:T(1024)}, s32[1024]{0:T(1024)S(1)}, u32[]{:S(2)}) copy-start(s32[1024]{0:T(1024)S(1)} %pad_clamp_fusion.4) | copy-start | bytes 12292
  18.9 139.8 %copy-start.7 = (s32[1024]{0:T(1024)}, s32[1024]{0:T(1024)S(1)}, u32[]{:S(2)}) copy-start(s32[1024]{0:T(1024)S(1)} %pad_clamp_fusion.3) | copy-start | bytes 12292
  19.0 143.0 %copy-start.8 = (s32[1024]{0:T(1024)}, s32[1024]{0:T(1024)S(1)}, u32[]{:S(2)}) copy-start(s32[1024]{0:T(1024)S(1)} %pad_clamp_fusion.2) | copy-start | bytes 12292
  19.0 145.5 %copy-start.9 = (s32[1024]{0:T(1024)}, s32[1024]{0:T(1024)S(1)}, u32[]{:S(2)}) copy-start(s32[1024]{0:T(1024)S(1)} %pad_clamp_fusion.1) | copy-start | bytes 12292
  19.0 148.0 %copy-start.10 = (s32[1024]{0:T(1024)}, s32[1024]{0:T(1024)S(1)}, u32[]{:S(2)}) copy-start(s32[1024]{0:T(1024)S(1)} %pad_clamp_fusion) | copy-start | bytes 12292
  54.5 9.1 %collective-permute-start.4 = (f32[512,1,1,128]{3,0,2,1:T(8,128)S(1)}, f32[512,1,1,128]{3,0,2,1:T(8,128)S(1)}, u32[]{:S(2)}, u32[]{:S(2)}) collective-permute-start(f32[512,1,1,128]{3,0,2,1:T(8,128)S(1)} %get-tuple-element.35), channel_id=1, source_target_pairs={{0,4},{4,8},{8,12},{12,16},{16,20},{20,24},{24,28},{28,32},{32,36}... | collective-permute-start | bytes 786440 | tf_op jit(solution)/shard_map/ppermute | solution.py:15
  60.3 7.7 %collective-permute-start.5 = (f32[512,1,1,128]{3,0,2,1:T(8,128)S(1)}, f32[512,1,1,128]{3,0,2,1:T(8,128)S(1)}, u32[]{:S(2)}, u32[]{:S(2)}) collective-permute-start(f32[512,1,1,128]{3,0,2,1:T(8,128)S(1)} %get-tuple-element.36), channel_id=1, source_target_pairs={{4,0},{8,4},{12,8},{16,12},{20,16},{24,20},{28,24},{32,28},{36,32}... | collective-permute-start | bytes 786440 | tf_op jit(solution)/shard_map/ppermute | solution.py:18
  68.1 22.2 %collective-permute-start.6 = (f32[512,1,4,128]{3,0,2,1:T(8,128)S(1)}, f32[512,1,4,128]{3,0,2,1:T(8,128)S(1)}, u32[]{:S(2)}, u32[]{:S(2)}) collective-permute-start(f32[512,1,4,128]{3,0,2,1:T(8,128)S(1)} %pad_maximum_fusion.4), channel_id=1, source_target_pairs={{0,1},{1,2},{2,3},{4,5},{5,6},{6,7},{8,9},{9,10},{10,11},{12,13},{... | collective-permute-start | bytes 3145736 | tf_op jit(solution)/shard_map/ppermute | solution.py:15
  71.2 23.3 %collective-permute-start.7 = (f32[512,1,4,128]{3,0,2,1:T(8,128)S(1)}, f32[512,1,4,128]{3,0,2,1:T(8,128)S(1)}, u32[]{:S(2)}, u32[]{:S(2)}) collective-permute-start(f32[512,1,4,128]{3,0,2,1:T(8,128)S(1)} %pad_maximum_fusion.4), channel_id=1, source_target_pairs={{1,0},{2,1},{3,2},{5,4},{6,5},{7,6},{9,8},{10,9},{11,10},{13,12},{... | collective-permute-start | bytes 3145736 | tf_op jit(solution)/shard_map/ppermute | solution.py:18
  114.0 9.1 %collective-permute-start.8 = (f32[512,1,1,128]{3,0,2,1:T(8,128)S(1)}, f32[512,1,1,128]{3,0,2,1:T(8,128)S(1)}, u32[]{:S(2)}, u32[]{:S(2)}) collective-permute-start(f32[512,1,1,128]{3,0,2,1:T(8,128)S(1)} %get-tuple-element.33), channel_id=1, source_target_pairs={{0,4},{4,8},{8,12},{12,16},{16,20},{20,24},{24,28},{28,32},{32,36}... | collective-permute-start | bytes 786440 | tf_op jit(solution)/shard_map/ppermute | solution.py:15
  119.7 7.7 %collective-permute-start.9 = (f32[512,1,1,128]{3,0,2,1:T(8,128)S(1)}, f32[512,1,1,128]{3,0,2,1:T(8,128)S(1)}, u32[]{:S(2)}, u32[]{:S(2)}) collective-permute-start(f32[512,1,1,128]{3,0,2,1:T(8,128)S(1)} %get-tuple-element.34), channel_id=1, source_target_pairs={{4,0},{8,4},{12,8},{16,12},{20,16},{24,20},{28,24},{32,28},{36,32}... | collective-permute-start | bytes 786440 | tf_op jit(solution)/shard_map/ppermute | solution.py:18
  127.5 21.9 %collective-permute-start.10 = (f32[512,1,4,128]{3,0,2,1:T(8,128)S(1)}, f32[512,1,4,128]{3,0,2,1:T(8,128)S(1)}, u32[]{:S(2)}, u32[]{:S(2)}) collective-permute-start(f32[512,1,4,128]{3,0,2,1:T(8,128)S(1)} %pad_maximum_fusion.5), channel_id=1, source_target_pairs={{0,1},{1,2},{2,3},{4,5},{5,6},{6,7},{8,9},{9,10},{10,11},{12,13},{... | collective-permute-start | bytes 3145736 | tf_op jit(solution)/shard_map/ppermute | solution.py:15
  130.3 23.3 %collective-permute-start.11 = (f32[512,1,4,128]{3,0,2,1:T(8,128)S(1)}, f32[512,1,4,128]{3,0,2,1:T(8,128)S(1)}, u32[]{:S(2)}, u32[]{:S(2)}) collective-permute-start(f32[512,1,4,128]{3,0,2,1:T(8,128)S(1)} %pad_maximum_fusion.5), channel_id=1, source_target_pairs={{1,0},{2,1},{3,2},{5,4},{6,5},{7,6},{9,8},{10,9},{11,10},{13,12},{... | collective-permute-start | bytes 3145736 | tf_op jit(solution)/shard_map/ppermute | solution.py:18
  174.9 8.1 %collective-permute-start.12 = (f32[512,1,1,128]{3,0,2,1:T(8,128)S(1)}, f32[512,1,1,128]{3,0,2,1:T(8,128)S(1)}, u32[]{:S(2)}, u32[]{:S(2)}) collective-permute-start(f32[512,1,1,128]{3,0,2,1:T(8,128)S(1)} %get-tuple-element.31), channel_id=1, source_target_pairs={{0,4},{4,8},{8,12},{12,16},{16,20},{20,24},{24,28},{28,32},{32,36}... | collective-permute-start | bytes 786440 | tf_op jit(solution)/shard_map/ppermute | solution.py:15
  179.7 7.7 %collective-permute-start.13 = (f32[512,1,1,128]{3,0,2,1:T(8,128)S(1)}, f32[512,1,1,128]{3,0,2,1:T(8,128)S(1)}, u32[]{:S(2)}, u32[]{:S(2)}) collective-permute-start(f32[512,1,1,128]{3,0,2,1:T(8,128)S(1)} %get-tuple-element.32), channel_id=1, source_target_pairs={{4,0},{8,4},{12,8},{16,12},{20,16},{24,20},{28,24},{32,28},{36,32}... | collective-permute-start | bytes 786440 | tf_op jit(solution)/shard_map/ppermute | solution.py:18
  187.5 20.5 %collective-permute-start.14 = (f32[512,1,4,128]{3,0,2,1:T(8,128)S(1)}, f32[512,1,4,128]{3,0,2,1:T(8,128)}, u32[]{:S(2)}, u32[]{:S(2)}) collective-permute-start(f32[512,1,4,128]{3,0,2,1:T(8,128)S(1)} %pad_maximum_fusion.6), channel_id=1, source_target_pairs={{0,1},{1,2},{2,3},{4,5},{5,6},{6,7},{8,9},{9,10},{10,11},{12,13},{... | collective-permute-start | bytes 3145736 | tf_op jit(solution)/shard_map/ppermute | solution.py:15
  190.0 23.1 %collective-permute-start.15 = (f32[512,1,4,128]{3,0,2,1:T(8,128)S(1)}, f32[512,1,4,128]{3,0,2,1:T(8,128)}, u32[]{:S(2)}, u32[]{:S(2)}) collective-permute-start(f32[512,1,4,128]{3,0,2,1:T(8,128)S(1)} %pad_maximum_fusion.6), channel_id=1, source_target_pairs={{1,0},{2,1},{3,2},{5,4},{6,5},{7,6},{9,8},{10,9},{11,10},{13,12},{... | collective-permute-start | bytes 3145736 | tf_op jit(solution)/shard_map/ppermute | solution.py:18
  234.0 132.4 %copy-start.12 = (pred[8,8]{1,0:T(8,128)(4,1)S(1)}, pred[8,8]{1,0:T(8,128)(4,1)}, u32[]{:S(2)}) copy-start(pred[8,8]{1,0:T(8,128)(4,1)} %iota_compare_fusion) | copy-start | bytes 196
  234.0 132.5 %copy-start.11 = (pred[8,8]{1,0:T(8,128)(4,1)S(1)}, pred[8,8]{1,0:T(8,128)(4,1)}, u32[]{:S(2)}) copy-start(pred[8,8]{1,0:T(8,128)(4,1)} %iota_compare_fusion.1) | copy-start | bytes 196
  (5 other events, 23.5 us)
where the time goes:
time: 397 us; the launch traced here: 396 us
  blocking collectives  109 us (27%)
  waiting for transfers between devices  105 us (26%)
  other arithmetic  59.1 us (15%)
  local copies, waits for them, and re-layouts  54.3 us (14%)
  starting transfers between devices  45.9 us (12%)
  matrix products  22.2 us (6%)
    psum x1, blocking collectives, body(): gram_mat = lax.psum(partial_gram, ('wide', 'grp')) / node_count  82.8 us
    ppermute x8, waiting for transfers between devices, with_halo(): lax.ppermute(lax.slice_in_dim(block, block.shape[dim] - width, None, axis...  71.7 us
    gather x20, local copies, waits for them, and re-layouts, combine_slots(): picked = jnp.take(flat_ext, position, axis=1)  47.7 us
    another operation x4, other arithmetic, mixing(): lower = jnp.linalg.cholesky(gram_mat)  47.6 us
    ppermute x8, waiting for transfers between devices, with_halo(): lax.ppermute(lax.slice_in_dim(block, 0, width, axis=dim), axis, backward)  33.2 us
    ppermute x8, starting transfers between devices, with_halo(): lax.ppermute(lax.slice_in_dim(block, block.shape[dim] - width, None, axis...  32.9 us
    all_to_all x1, blocking collectives, body(): lax.all_to_all(mixed_rows.reshape(current.shape), 'wide', split_axis=0, c...  25.8 us
    dot_general x20, matrix products, combine_slots(): jnp.einsum('rij,srj->sri', weights_here, picked, precision=lax.Precision....  20.4 us
  transfers between devices with their start and end apart: 16, of which 15 were waited for; matrix products, arithmetic and copies ran while one was open for 1% of the time, Pallas kernels for 0%

commit v1 on v0

v1 whole, which is shorter than its diff:
```python
import functools

import jax
import jax.numpy as jnp
from jax import lax
from jax.experimental import pallas as pl
from jax.experimental.pallas import tpu as pltpu
from jax.sharding import PartitionSpec as P

MESH = pl.DeviceIdType.MESH
F32 = jnp.float32
BF16 = jnp.bfloat16
VEC = 8
DEG = 4
BS = 128
K = 5
G = 4
PAIRS = [(a, c) for a in range(VEC) for c in range(a + 1)]
PAIR_ROWS = 40


def split(value):
    high = value.astype(BF16)
    low = (value - high.astype(F32)).astype(BF16)
    return high, low


def kernel(
    wide,
    nodes,
    slab,
    hblocks,
    codes,
    rotation,
    out,
    slab_in,
    h_in,
    codes_in,
    codes_sm,
    hs,
    fields,
    halo,
    xs,
    fin,
    recv,
    gram,
    rot_in,
    rot_wide,
    mixer,
    local_sem,
    slab_send,
    slab_recv,
    codes_send,
    codes_recv,
    h_send,
    h_recv,
    halo_send,
    halo_recv,
    fin_send,
    fin_recv,
    gram_send,
    gram_recv,
):
    w = lax.axis_index("wide")
    g = lax.axis_index("grp")
    nb = wide // G
    chunk = VEC * nb
    source = w // nb
    is_own = source == g
    has_left = w > 0
    has_right = w < wide - 1

    def remote(src, dst, send_sem, recv_sem, to):
        return pltpu.make_async_remote_copy(
            src_ref=src, dst_ref=dst, send_sem=send_sem, recv_sem=recv_sem, device_id=to, device_id_type=MESH
        )

    def arrived(ref, sem):
        pltpu.make_async_copy(ref, ref, sem).wait()

    def row_at(d):
        return lax.rem(g + d, G)

    barrier = pltpu.get_barrier_semaphore()
    for d in range(1, G):
        pl.semaphore_signal(barrier, inc=1, device_id=(w, row_at(d)), device_id_type=MESH)

    @pl.when(has_left)
    def _():
        pl.semaphore_signal(barrier, inc=1, device_id=(w - 1, g), device_id_type=MESH)

    @pl.when(has_right)
    def _():
        pl.semaphore_signal(barrier, inc=1, device_id=(w + 1, g), device_id_type=MESH)

    @pl.loop(0, wide)
    def _(i):
        @pl.when(jnp.logical_not(jnp.logical_and(i == w, is_own)))
        def _():
            pl.semaphore_signal(barrier, inc=1, device_id=(i, source), device_id_type=MESH)

    own_slab = pltpu.make_async_copy(slab.at[pl.ds(g * 2 * chunk, 2 * chunk)], slab_in.at[g], local_sem.at[0])
    own_slab.start()
    own_h = pltpu.make_async_copy(hblocks, h_in.at[g], local_sem.at[1])
    own_h.start()
    own_codes = pltpu.make_async_copy(codes, codes_in.at[g], local_sem.at[2])
    own_codes.start()
    own_rot = pltpu.make_async_copy(rotation.at[w], rot_in, local_sem.at[3])
    own_rot.start()

    zero = jnp.zeros((2 * chunk, BS), BF16)
    for parity in range(2):
        for col in range(4):
            xs[parity, col] = zero
            xs[parity, 20 + col] = zero

        @pl.when(jnp.logical_not(has_left))
        def _():
            for r in range(G):
                xs[parity, (r + 1) * 4] = zero

        @pl.when(jnp.logical_not(has_right))
        def _():
            for r in range(G):
                xs[parity, (r + 1) * 4 + 3] = zero

    peers = G - 1 + wide - is_own.astype(jnp.int32) + has_left.astype(jnp.int32) + has_right.astype(jnp.int32)
    pl.semaphore_wait(barrier, peers)

    def slab_copy(d):
        to = row_at(d)
        return remote(
            slab.at[pl.ds(to * 2 * chunk, 2 * chunk)], slab_in.at[g], slab_send.at[d], slab_recv.at[g], (w, to)
        )

    def codes_copy(d):
        return remote(codes, codes_in.at[g], codes_send.at[d], codes_recv.at[g], (w, row_at(d)))

    def h_copy(half, d):
        return remote(
            hblocks.at[half], h_in.at[g, half], h_send.at[half, d // 2], h_recv.at[g, half], (w, row_at(d))
        )

    def h_forward(half, d):
        origin = row_at(G - d)
        return remote(
            h_in.at[origin, half], h_in.at[origin, half], h_send.at[half, 2], h_recv.at[origin, half], (w, row_at(d))
        )

    for d in (1, 3, 2):
        slab_copy(d).start()
    for d in (1, 3, 2):
        codes_copy(d).start()
    h_copy(0, 1).start()
    h_copy(1, 3).start()
    h_copy(1, 1).start()
    h_copy(0, 3).start()

    def split_h(r):
        @pl.loop(0, 2)
        def _(q):
            for k in range(K):
                high, low = split(h_in[r, q, k])
                hs[r, q, 0:BS, k * BS : (k + 1) * BS] = high
                hs[r, q, BS : 2 * BS, k * BS : (k + 1) * BS] = low

    def store_split(parity, position, value):
        high, low = split(value)
        xs[parity, position, 0:chunk] = high
        xs[parity, position, chunk : 2 * chunk] = low

    def halo_copy(n, r, side):
        to = w - 1 if side == 0 else w + 1
        return remote(
            fields.at[n, r, side],
            halo.at[n, r, 1 - side],
            halo_send.at[n, r, side],
            halo_recv.at[n, r, 1 - side],
            (to, g),
        )

    def send_halos(n, r):
        @pl.when(has_left)
        def _():
            halo_copy(n, r, 0).start()

        @pl.when(has_right)
        def _():
            halo_copy(n, r, 1).start()

    def take_halos(n):
        parity = n % 2

        @pl.loop(0, G)
        def _(r):
            @pl.when(has_left)
            def _():
                halo_copy(n, r, 1).wait_recv()
                store_split(parity, (r + 1) * 4, halo[n, r, 0])

            @pl.when(has_right)
            def _():
                halo_copy(n, r, 0).wait_recv()
                store_split(parity, (r + 1) * 4 + 3, halo[n, r, 1])

    def product(n, r, q):
        parity = n % 2
        picked = [xs[parity, r * 4 + q + codes_sm[r, q, k]] for k in range(K)]
        both = jnp.concatenate(picked, axis=1)
        p = lax.dot_general(both, hs[r, q], (((1,), (1,)), ((), ())), preferred_element_type=F32)
        small = p[:chunk, BS:] + p[chunk:, :BS] + p[chunk:, BS:]
        return p[:chunk, :BS] + small

    def apply_row(n, r):
        for q in range(2):
            value = product(n, r, q)
            if n > 0:
                value = 2.0 * value - fields[n - 1, r, q]
            if n + 1 < DEG:
                fields[n + 1, r, q] = value
                store_split((n + 1) % 2, (r + 1) * 4 + 1 + q, value)
            else:
                fin[r, :, q * VEC : (q + 1) * VEC, :] = value.reshape(nb, VEC, BS)
        if n + 1 < DEG:
            send_halos(n + 1, r)

    own_h.wait()
    split_h(g)
    own_rot.wait()
    rot = rot_in[...]
    for c in range(VEC):
        for a in range(VEC):
            rot_wide[c * VEC + a] = jnp.broadcast_to(rot[c : c + 1, a : a + 1], (VEC, BS))

    def start_row(r):
        for q in range(2):
            value = slab_in[r, pl.ds(q, chunk, stride=2), :]
            fields[0, r, q] = value
            store_split(0, (r + 1) * 4 + 1 + q, value)
        send_halos(0, r)

    own_slab.wait()
    start_row(g)
    for d in (1, 3, 2):
        arrived(slab_in.at[row_at(d)], slab_recv.at[row_at(d)])
        start_row(row_at(d))

    own_codes.wait()
    for d in (1, 3, 2):
        arrived(codes_in.at[row_at(d)], codes_recv.at[row_at(d)])
    to_scalars = pltpu.make_async_copy(codes_in, codes_sm, local_sem.at[4])
    to_scalars.start()
    to_scalars.wait()

    def h_wait(d, half):
        r = row_at(d)
        arrived(h_in.at[r, half], h_recv.at[r, half])

    take_halos(0)
    apply_row(0, g)
    h_wait(3, 0)
    h_forward(0, 1).start()
    h_wait(1, 1)
    h_forward(1, 3).start()
    h_wait(3, 1)
    split_h(row_at(3))
    apply_row(0, row_at(3))
    h_wait(1, 0)
    split_h(row_at(1))
    apply_row(0, row_at(1))
    h_wait(2, 0)
    h_wait(2, 1)
    split_h(row_at(2))
    apply_row(0, row_at(2))

    for n in range(1, DEG - 1):
        take_halos(n)

        @pl.loop(0, G)
        def _(r):
            apply_row(n, r)

    take_halos(DEG - 1)

    @pl.loop(0, G)
    def _(d):
        r = row_at(d)
        apply_row(DEG - 1, r)

        @pl.loop(0, nb)
        def _(i):
            b = lax.rem(i + w, nb)
            to = g * nb + b
            own = jnp.logical_and(to == w, r == g)

            @pl.when(jnp.logical_not(own))
            def _():
                remote(
                    fin.at[r, b], recv.at[pl.ds(w * 2 * VEC, 2 * VEC)], fin_send.at[0], fin_recv.at[0], (to, r)
                ).start()

            @pl.when(own)
            def _():
                pltpu.make_async_copy(
                    fin.at[r, b], recv.at[pl.ds(w * 2 * VEC, 2 * VEC)], fin_recv.at[0]
                ).start()

    arrived(recv, fin_recv.at[0])

    groups = 2 * wide // VEC

    def tiles(group):
        return [recv[pl.ds(group * VEC * VEC + s, VEC, stride=VEC), :] for s in range(VEC)]

    def add(group, sums):
        x = tiles(group)
        return tuple(total + x[a] * x[c] for total, (a, c) in zip(sums, PAIRS))

    sums = lax.fori_loop(0, groups, add, tuple(jnp.zeros((VEC, BS), F32) for _ in PAIRS))
    for i, total in enumerate(sums):
        gram[g, i : i + 1, :] = jnp.sum(total, axis=0, keepdims=True)
    for i in range(len(PAIRS), PAIR_ROWS):
        gram[g, i : i + 1, :] = jnp.zeros((1, BS), F32)

    def gram_copy(d):
        return remote(gram.at[g], gram.at[g], gram_send.at[d], gram_recv.at[g], (w, row_at(d)))

    for d in (1, 3, 2):
        gram_copy(d).start()
    for d in (1, 3, 2):
        arrived(gram.at[row_at(d)], gram_recv.at[row_at(d)])
    whole = (gram[0] + gram[1]) + (gram[2] + gram[3])
    whole = jnp.sum(whole, axis=1, keepdims=True) * (1.0 / nodes)
    entry = {pair: jnp.broadcast_to(whole[i : i + 1, :], (VEC, BS)) for i, pair in enumerate(PAIRS)}
    lower, inverse = {}, []
    for j in range(VEC):
        rest = entry[j, j]
        for k in range(j):
            rest = rest - lower[j, k] * lower[j, k]
        root = lax.rsqrt(rest)
        root = root * (1.5 - 0.5 * rest * root * root)
        inverse.append(root)
        for i in range(j + 1, VEC):
            value = entry[i, j]
            for k in range(j):
                value = value - lower[i, k] * lower[j, k]
            lower[i, j] = value * root
    for a in range(VEC):
        row = {}
        for c in reversed(range(VEC)):
            value = rot_wide[c * VEC + a]
            for k in range(c + 1, VEC):
                value = value - row[k] * lower[k, c]
            row[c] = value * inverse[c]
            mixer[a * VEC + c] = row[c]

    @pl.loop(0, groups)
    def _(group):
        x = tiles(group)
        for a in range(VEC):
            value = mixer[a * VEC] * x[0]
            for c in range(1, VEC):
                value = value + mixer[a * VEC + c] * x[c]
            out[a, 0, pl.ds(pl.multiple_of(group * VEC, VEC), VEC), :] = value

    for d in range(1, G):
        slab_copy(d).wait_send()
        codes_copy(d).wait_send()
        gram_copy(d).wait_send()
    for half in range(2):
        h_copy(half, 1).wait_send()
        h_copy(half, 3).wait_send()
    h_forward(0, 1).wait_send()
    h_forward(1, 3).wait_send()

    @pl.loop(0, DEG)
    def _(n):
        @pl.loop(0, G)
        def _(r):
            @pl.when(has_left)
            def _():
                halo_copy(n, r, 0).wait_send()

            @pl.when(has_right)
            def _():
                halo_copy(n, r, 1).wait_send()

    @pl.when(is_own)
    def _():
        part = recv.at[pl.ds(0, (wide - 1) * 2 * VEC)]
        pltpu.make_async_copy(part, part, fin_send.at[0]).wait()

    @pl.when(jnp.logical_not(is_own))
    def _():
        pltpu.make_async_copy(recv, recv, fin_send.at[0]).wait()


def body(slab, hblocks, blist, rotation):
    wide = lax.axis_size("wide")
    states = slab.shape[0]
    chunk = states // G
    nb = wide // G
    nodes = G * 2 * wide * BS
    offsets = (blist // 3) * 4 + blist % 3
    codes = jnp.pad(offsets.reshape(2, K), ((0, 6), (0, BS - K)))
    dma = pltpu.SemaphoreType.DMA
    any_space = pl.BlockSpec(memory_space=pl.ANY)
    return pl.pallas_call(
        functools.partial(kernel, wide, nodes),
        out_shape=jax.ShapeDtypeStruct((VEC, 1, 2 * wide, BS), F32),
        in_specs=[any_space, any_space, any_space, any_space],
        out_specs=pl.BlockSpec(memory_space=pltpu.VMEM),
        scratch_shapes=[
            pltpu.VMEM((G, 2 * chunk, BS), F32),
            pltpu.VMEM((G, 2, K, BS, BS), F32),
            pltpu.VMEM((G, 8, BS), jnp.int32),
            pltpu.SMEM((G, 8, BS), jnp.int32),
            pltpu.VMEM((G, 2, 2 * BS, K * BS), BF16),
            pltpu.VMEM((DEG, G, 2, chunk, BS), F32),
            pltpu.VMEM((DEG, G, 2, chunk, BS), F32),
            pltpu.VMEM((2, 24, 2 * chunk, BS), BF16),
            pltpu.VMEM((G, nb, 2 * VEC, BS), F32),
            pltpu.VMEM((wide * 2 * VEC, BS), F32),
            pltpu.VMEM((G, PAIR_ROWS, BS), F32),
            pltpu.VMEM((VEC, VEC), F32),
            pltpu.VMEM((VEC * VEC, VEC, BS), F32),
            pltpu.VMEM((VEC * VEC, VEC, BS), F32),
            dma((5,)),
            dma((G,)),
            dma((G,)),
            dma((G,)),
            dma((G,)),
            dma((2, 3)),
            dma((G, 2)),
            dma((DEG, G, 2)),
            dma((DEG, G, 2)),
            dma((1,)),
            dma((1,)),
            dma((G,)),
            dma((G,)),
        ],
        compiler_params=pltpu.CompilerParams(
            collective_id=0, has_side_effects=True, vmem_limit_bytes=40 * 1024 * 1024
        ),
        cost_estimate=pl.CostEstimate(flops=3 * 10**9, bytes_accessed=2 * 1024 * 1024, transcendentals=0),
    )(slab.reshape(2 * states, BS), hblocks.reshape(2, K, BS, BS), codes, rotation)


def solution(mesh):
    in_specs = (
        P(None, "grp", "wide", None),
        P("grp", "wide", None, None, None),
        P("grp", "wide", None),
        P(),
    )
    out_specs = P("wide", "grp", None, None)
    return jax.shard_map(body, mesh=mesh, in_specs=in_specs, out_specs=out_specs, check_vma=False)
```

time: 397 us -> 84.2 us (0.21)
  blocking collectives: 109 us -> 0 us
  waiting for transfers between devices: 105 us -> 0 us
  Pallas kernels: 0 us -> 79.4 us
  other arithmetic: 59.1 us -> 0.02 us
  local copies, waits for them, and re-layouts: 54.3 us -> 4.51 us
  starting transfers between devices: 45.9 us -> 0 us
  matrix products: 22.2 us -> 0 us
    ppermute x16 -> x0, waiting for transfers between devices: 105 us -> none  [the longest x8 71.7 us: with_halo(): lax.ppermute(lax.slice_in_dim(block, block.shape[dim] - width, None, axis...]
    psum x1 -> x0, blocking collectives: 82.8 us -> none  [body(): gram_mat = lax.psum(partial_gram, ('wide', 'grp')) / node_count]
    pallas_call x0 -> x1, Pallas kernels: none -> 79.4 us  [body(): pl.pallas_call(functools.partial(kernel, wide, nodes), out_shape=jax.Shap...]
    another operation x7 -> x0, other arithmetic: 49 us -> none  [the longest x4 47.6 us: mixing(): lower = jnp.linalg.cholesky(gram_mat)]
    gather x20 -> x0, local copies, waits for them, and re-layouts: 47.7 us -> none  [combine_slots(): picked = jnp.take(flat_ext, position, axis=1)]
    ppermute x16 -> x0, starting transfers between devices: 45.9 us -> none  [the longest x8 32.9 us: with_halo(): lax.ppermute(lax.slice_in_dim(block, block.shape[dim] - width, None, axis...]
    all_to_all x1 -> x0, blocking collectives: 25.8 us -> none  [body(): lax.all_to_all(mixed_rows.reshape(current.shape), 'wide', split_axis=0, c...]
    dot_general x22 -> x0, matrix products: 21.5 us -> none  [the longest x20 20.4 us: combine_slots(): jnp.einsum('rij,srj->sri', weights_here, picked, precision=lax.Precision....]
  transfers between devices with their start and end apart: 16 -> 0, of which waited for: 15 -> 0; matrix products, arithmetic and copies ran while one was open for 1% -> 0% of each run, Pallas kernels for 0% -> 0%
where the time goes in v1:
time: 84.2 us; the launch traced here: 83.9 us
  Pallas kernels  79.4 us (94%)
  local copies, waits for them, and re-layouts  4.51 us (5%)
    pallas_call x1, Pallas kernels, body(): pl.pallas_call(functools.partial(kernel, wide, nodes), out_shape=jax.Shap...  79.4 us
    unnamed x8, local copies, waits for them, and re-layouts  4.51 us

profile of v1, /device:TPU:1, one launch (start us, length us, event | category | flops | bytes accessed | tf_op | source)
XLA Modules:
  0.0 83.9 jit_solution(14323863541669392593)
XLA Ops:
  0.0 0.0 copy-start.2
  0.0 0.7 copy-done.2
  0.7 0.9 %copy.5.rotation = f32[64,8,8]{2,1,0:T(8,128)S(1)} copy(f32[64,8,8]{0,2,1:T(8,128)} %param.7) | data formatting | bytes 32768 | tf_op args[3]
  1.6 0.0 copy-start
  1.6 1.1 %copy-done = f32[1,2,5,128,128]{4,3,2,1,0:T(8,128)S(1)} copy-done((f32[1,2,5,128,128]{4,3,2,1,0:T(8,128)S(1)}, f32[1,2,5,128,128]{4,3,2,1,0:T(8,128)}, u32[]{:S(2)}) %copy-start) | copy-done | bytes 655384
  2.7 0.0 copy-start.1
  2.7 1.0 %copy-done.1 = f32[512,1,2,128]{3,2,1,0:T(2,128)S(1)} copy-done((f32[512,1,2,128]{3,2,1,0:T(2,128)S(1)}, f32[512,1,2,128]{3,2,1,0:T(2,128)}, u32[]{:S(2)}) %copy-start.1) | copy-done | bytes 524312
  3.8 79.4 %shard_map.46 = f32[8,1,128,128]{3,2,1,0:T(8,128)S(1)} custom-call(f32[1024,128]{1,0:T(8,128)S(1)} %bitcast.5, f32[2,5,128,128]{3,2,1,0:T(8,128)S(1)} %bitcast.4, s32[8,128]{1,0:T(8,128)S(1)} %pad.4.codes, f32[64,8,8]{2,1,0:T(8,128)S(1)} %copy.5.rotation), custom_call_target="tpu_custom_call" | custom-call | flops 3000000000 | bytes 2097152 | tf_op jit(solution)/shard_map/pallas_call | solution.py:408
  83.1 0.8 copy.7
  (2 shorter events, 0.0 us)
Async XLA Ops:
  0.0 0.7 copy-start.2
  1.6 1.1 %copy-start = (f32[1,2,5,128,128]{4,3,2,1,0:T(8,128)S(1)}, f32[1,2,5,128,128]{4,3,2,1,0:T(8,128)}, u32[]{:S(2)}) copy-start(f32[1,2,5,128,128]{4,3,2,1,0:T(8,128)} %param.5) | copy-start | bytes 1966084
  2.7 1.0 %copy-start.1 = (f32[512,1,2,128]{3,2,1,0:T(2,128)S(1)}, f32[512,1,2,128]{3,2,1,0:T(2,128)}, u32[]{:S(2)}) copy-start(f32[512,1,2,128]{3,2,1,0:T(2,128)} %param.4) | copy-start | bytes 1572868

commit v2 on v1

--- a/solution.py
+++ b/solution.py
@@ -15,14 +15,20 @@
 BS = 128
 K = 5
 G = 4
-PAIRS = [(a, c) for a in range(VEC) for c in range(a + 1)]
-PAIR_ROWS = 40
 
 
 def split(value):
     high = value.astype(BF16)
     low = (value - high.astype(F32)).astype(BF16)
     return high, low
+
+
+def reach_steps(wide):
+    steps, reach = [], 1
+    while 2 * reach < wide:
+        steps.append(reach)
+        reach *= 2
+    return steps
 
 
 def kernel(
@@ -30,20 +36,24 @@
     nodes,
     slab,
     hblocks,
-    codes,
+    blist,
     rotation,
     out,
     slab_in,
     h_in,
     codes_in,
     codes_sm,
+    position_sm,
     hs,
     fields,
     halo,
     xs,
     fin,
     recv,
-    gram,
+    both_last,
+    gram_all,
+    gram_out,
+    gram_in,
     rot_in,
     rot_wide,
     mixer,
@@ -60,11 +70,13 @@
     fin_recv,
     gram_send,
     gram_recv,
+    reach_sem,
 ):
     w = lax.axis_index("wide")
     g = lax.axis_index("grp")
     nb = wide // G
     chunk = VEC * nb
+    steps = reach_steps(wide)
     source = w // nb
     is_own = source == g
     has_left = w > 0
@@ -81,31 +93,23 @@
     def row_at(d):
         return lax.rem(g + d, G)
 
+    def at_offset(d):
+        return lax.rem(w + d, wide)
+
     barrier = pltpu.get_barrier_semaphore()
     for d in range(1, G):
         pl.semaphore_signal(barrier, inc=1, device_id=(w, row_at(d)), device_id_type=MESH)
 
-    @pl.when(has_left)
-    def _():
-        pl.semaphore_signal(barrier, inc=1, device_id=(w - 1, g), device_id_type=MESH)
-
-    @pl.when(has_right)
-    def _():
-        pl.semaphore_signal(barrier, inc=1, device_id=(w + 1, g), device_id_type=MESH)
-
-    @pl.loop(0, wide)
-    def _(i):
-        @pl.when(jnp.logical_not(jnp.logical_and(i == w, is_own)))
-        def _():
-            pl.semaphore_signal(barrier, inc=1, device_id=(i, source), device_id_type=MESH)
+    for to in (at_offset(1), at_offset(wide - 1)):
+        pl.semaphore_signal(barrier, inc=1, device_id=(to, g), device_id_type=MESH)
 
     own_slab = pltpu.make_async_copy(slab.at[pl.ds(g * 2 * chunk, 2 * chunk)], slab_in.at[g], local_sem.at[0])
     own_slab.start()
     own_h = pltpu.make_async_copy(hblocks, h_in.at[g], local_sem.at[1])
     own_h.start()
-    own_codes = pltpu.make_async_copy(codes, codes_in.at[g], local_sem.at[2])
+    own_codes = pltpu.make_async_copy(blist.at[0], codes_in.at[g], local_sem.at[2])
     own_codes.start()
-    own_rot = pltpu.make_async_copy(rotation.at[w], rot_in, local_sem.at[3])
+    own_rot = pltpu.make_async_copy(rotation, rot_in, local_sem.at[3])
     own_rot.start()
 
     zero = jnp.zeros((2 * chunk, BS), BF16)
@@ -124,8 +128,18 @@
             for r in range(G):
                 xs[parity, (r + 1) * 4 + 3] = zero
 
-    peers = G - 1 + wide - is_own.astype(jnp.int32) + has_left.astype(jnp.int32) + has_right.astype(jnp.int32)
-    pl.semaphore_wait(barrier, peers)
+    pl.semaphore_wait(barrier, G + 1)
+
+    def greet(i):
+        for to in (at_offset(steps[i]), at_offset(wide - steps[i])):
+            pl.semaphore_signal(reach_sem.at[i], inc=1, device_id=(to, g), device_id_type=MESH)
+
+    def greeted(i):
+        pl.semaphore_wait(reach_sem.at[i], 2)
+        if i + 1 < len(steps):
+            greet(i + 1)
+
+    greet(0)
 
     def slab_copy(d):
         to = row_at(d)
@@ -134,7 +148,7 @@
         )
 
     def codes_copy(d):
-        return remote(codes, codes_in.at[g], codes_send.at[d], codes_recv.at[g], (w, row_at(d)))
+        return remote(blist.at[0], codes_in.at[g], codes_send.at[d], codes_recv.at[g], (w, row_at(d)))
 
     def h_copy(half, d):
         return remote(
@@ -205,7 +219,7 @@
 
     def product(n, r, q):
         parity = n % 2
-        picked = [xs[parity, r * 4 + q + codes_sm[r, q, k]] for k in range(K)]
+        picked = [xs[parity, r * 4 + position_sm[r, q * 8 + k]] for k in range(K)]
         both = jnp.concatenate(picked, axis=1)
         p = lax.dot_general(both, hs[r, q], (((1,), (1,)), ((), ())), preferred_element_type=F32)
         small = p[:chunk, BS:] + p[chunk:, :BS] + p[chunk:, BS:]
@@ -221,16 +235,20 @@
                 store_split((n + 1) % 2, (r + 1) * 4 + 1 + q, value)
             else:
                 fin[r, :, q * VEC : (q + 1) * VEC, :] = value.reshape(nb, VEC, BS)
+                high, low = split(value)
+                both_last[0:chunk, q * BS : (q + 1) * BS] = high
+                both_last[chunk : 2 * chunk, q * BS : (q + 1) * BS] = low
         if n + 1 < DEG:
             send_halos(n + 1, r)
 
     own_h.wait()
     split_h(g)
     own_rot.wait()
-    rot = rot_in[...]
+    mine = lax.broadcasted_iota(jnp.int32, (VEC, wide), 1) == w
     for c in range(VEC):
+        column = jnp.sum(jnp.where(mine, rot_in[c], 0.0), axis=1, keepdims=True)
         for a in range(VEC):
-            rot_wide[c * VEC + a] = jnp.broadcast_to(rot[c : c + 1, a : a + 1], (VEC, BS))
+            rot_wide[c * VEC + a] = jnp.broadcast_to(column[a : a + 1, :], (VEC, BS))
 
     def start_row(r):
         for q in range(2):
@@ -251,23 +269,41 @@
     to_scalars = pltpu.make_async_copy(codes_in, codes_sm, local_sem.at[4])
     to_scalars.start()
     to_scalars.wait()
+    for r in range(G):
+        for q in range(2):
+            for k in range(K):
+                code = codes_sm[r, q, k]
+                line = (code * 11) >> 5
+                position_sm[r, q * 8 + k] = line * 4 + code - 3 * line + q
 
     def h_wait(d, half):
         r = row_at(d)
         arrived(h_in.at[r, half], h_recv.at[r, half])
 
+    waiting = list(range(len(steps)))
+
+    def next_round():
+        if waiting:
+            greeted(waiting.pop(0))
+
+    next_round()
     take_halos(0)
     apply_row(0, g)
+    next_round()
     h_wait(3, 0)
     h_forward(0, 1).start()
     h_wait(1, 1)
     h_forward(1, 3).start()
+    next_round()
     h_wait(3, 1)
     split_h(row_at(3))
     apply_row(0, row_at(3))
+    next_round()
     h_wait(1, 0)
     split_h(row_at(1))
     apply_row(0, row_at(1))
+    while waiting:
+        next_round()
     h_wait(2, 0)
     h_wait(2, 1)
     split_h(row_at(2))
@@ -282,11 +318,7 @@
 
     take_halos(DEG - 1)
 
-    @pl.loop(0, G)
-    def _(d):
-        r = row_at(d)
-        apply_row(DEG - 1, r)
-
+    def to_owners(r, block_copy, local_copy):
         @pl.loop(0, nb)
         def _(i):
             b = lax.rem(i + w, nb)
@@ -295,43 +327,62 @@
 
             @pl.when(jnp.logical_not(own))
             def _():
-                remote(
-                    fin.at[r, b], recv.at[pl.ds(w * 2 * VEC, 2 * VEC)], fin_send.at[0], fin_recv.at[0], (to, r)
-                ).start()
+                block_copy(b, (to, r)).start()
 
             @pl.when(own)
             def _():
-                pltpu.make_async_copy(
-                    fin.at[r, b], recv.at[pl.ds(w * 2 * VEC, 2 * VEC)], fin_recv.at[0]
-                ).start()
-
-    arrived(recv, fin_recv.at[0])
-
+                local_copy(b).start()
+
+    gram_all[...] = jnp.zeros_like(gram_all)
+
+    @pl.loop(0, G)
+    def _(d):
+        r = row_at(d)
+        apply_row(DEG - 1, r)
+        slot = recv.at[pl.ds(w * 2 * VEC, 2 * VEC)]
+        to_owners(
+            r,
+            lambda b, to: remote(fin.at[r, b], slot, fin_send.at[0], fin_recv.at[0], to),
+            lambda b: pltpu.make_async_copy(fin.at[r, b], slot, fin_recv.at[0]),
+        )
+        both = both_last[...]
+        gram_all[...] += lax.dot_general(both, both, (((1,), (1,)), ((), ())), preferred_element_type=F32)
+
+    states_gram = (gram_all[:chunk, chunk:] + gram_all[chunk:, :chunk] + gram_all[chunk:, chunk:]) + gram_all[:chunk, :chunk]
+    row_id = lax.broadcasted_iota(jnp.int32, (chunk, chunk), 0)
+    lane_id = lax.broadcasted_iota(jnp.int32, (chunk, chunk), 1)
+    states_gram = jnp.where(row_id // VEC == lane_id // VEC, states_gram, 0.0)
+    fold_row = lax.broadcasted_iota(jnp.int32, (chunk, BS), 0)
+    fold_lane = lax.broadcasted_iota(jnp.int32, (chunk, BS), 1)
+    fold = jnp.where(fold_row % VEC == fold_lane % VEC, 1.0, 0.0).astype(F32)
+    folded = jnp.dot(states_gram, fold, precision=lax.Precision.HIGHEST, preferred_element_type=F32)
+    folded = jnp.where(fold_row % VEC == fold_lane // VEC, folded, 0.0)
+    flat = jnp.sum(folded.reshape(nb, VEC, BS), axis=1)
+    for b in range(nb):
+        gram_out[b] = flat[b : b + 1, :]
+
+    @pl.loop(0, G)
+    def _(d):
+        r = row_at(d)
+        to_owners(
+            r,
+            lambda b, to: remote(gram_out.at[b], gram_in.at[w], gram_send.at[0], gram_recv.at[0], to),
+            lambda b: pltpu.make_async_copy(gram_out.at[b], gram_in.at[w], gram_recv.at[0]),
+        )
+
+    arrived(gram_in, gram_recv.at[0])
+    whole = jnp.sum(gram_in[...], axis=0) * (1.0 / nodes)
+
+    entry = {}
+    for a in range(VEC):
+        for c in range(a + 1):
+            i = a * VEC + c
+            entry[a, c] = jnp.broadcast_to(whole[:, i : i + 1], (VEC, BS))
     groups = 2 * wide // VEC
 
     def tiles(group):
         return [recv[pl.ds(group * VEC * VEC + s, VEC, stride=VEC), :] for s in range(VEC)]
 
-    def add(group, sums):
-        x = tiles(group)
-        return tuple(total + x[a] * x[c] for total, (a, c) in zip(sums, PAIRS))
-
-    sums = lax.fori_loop(0, groups, add, tuple(jnp.zeros((VEC, BS), F32) for _ in PAIRS))
-    for i, total in enumerate(sums):
-        gram[g, i : i + 1, :] = jnp.sum(total, axis=0, keepdims=True)
-    for i in range(len(PAIRS), PAIR_ROWS):
-        gram[g, i : i + 1, :] = jnp.zeros((1, BS), F32)
-
-    def gram_copy(d):
-        return remote(gram.at[g], gram.at[g], gram_send.at[d], gram_recv.at[g], (w, row_at(d)))
-
-    for d in (1, 3, 2):
-        gram_copy(d).start()
-    for d in (1, 3, 2):
-        arrived(gram.at[row_at(d)], gram_recv.at[row_at(d)])
-    whole = (gram[0] + gram[1]) + (gram[2] + gram[3])
-    whole = jnp.sum(whole, axis=1, keepdims=True) * (1.0 / nodes)
-    entry = {pair: jnp.broadcast_to(whole[i : i + 1, :], (VEC, BS)) for i, pair in enumerate(PAIRS)}
     lower, inverse = {}, []
     for j in range(VEC):
         rest = entry[j, j]
@@ -354,6 +405,8 @@
             row[c] = value * inverse[c]
             mixer[a * VEC + c] = row[c]
 
+    arrived(recv, fin_recv.at[0])
+
     @pl.loop(0, groups)
     def _(group):
         x = tiles(group)
@@ -366,7 +419,6 @@
     for d in range(1, G):
         slab_copy(d).wait_send()
         codes_copy(d).wait_send()
-        gram_copy(d).wait_send()
     for half in range(2):
         h_copy(half, 1).wait_send()
         h_copy(half, 3).wait_send()
@@ -388,11 +440,14 @@
     @pl.when(is_own)
     def _():
         part = recv.at[pl.ds(0, (wide - 1) * 2 * VEC)]
-        pltpu.make_async_copy(part, part, fin_send.at[0]).wait()
+        arrived(part, fin_send.at[0])
+        part = gram_in.at[pl.ds(0, wide - 1)]
+        arrived(part, gram_send.at[0])
 
     @pl.when(jnp.logical_not(is_own))
     def _():
-        pltpu.make_async_copy(recv, recv, fin_send.at[0]).wait()
+        arrived(recv, fin_send.at[0])
+        arrived(gram_in, gram_send.at[0])
 
 
 def body(slab, hblocks, blist, rotation):
@@ -401,8 +456,6 @@
     chunk = states // G
     nb = wide // G
     nodes = G * 2 * wide * BS
-    offsets = (blist // 3) * 4 + blist % 3
-    codes = jnp.pad(offsets.reshape(2, K), ((0, 6), (0, BS - K)))
     dma = pltpu.SemaphoreType.DMA
     any_space = pl.BlockSpec(memory_space=pl.ANY)
     return pl.pallas_call(
@@ -413,16 +466,20 @@
         scratch_shapes=[
             pltpu.VMEM((G, 2 * chunk, BS), F32),
             pltpu.VMEM((G, 2, K, BS, BS), F32),
-            pltpu.VMEM((G, 8, BS), jnp.int32),
-            pltpu.SMEM((G, 8, BS), jnp.int32),
+            pltpu.VMEM((G, 2, K), jnp.int32),
+            pltpu.SMEM((G, 2, K), jnp.int32),
+            pltpu.SMEM((G, 16), jnp.int32),
             pltpu.VMEM((G, 2, 2 * BS, K * BS), BF16),
             pltpu.VMEM((DEG, G, 2, chunk, BS), F32),
             pltpu.VMEM((DEG, G, 2, chunk, BS), F32),
             pltpu.VMEM((2, 24, 2 * chunk, BS), BF16),
             pltpu.VMEM((G, nb, 2 * VEC, BS), F32),
             pltpu.VMEM((wide * 2 * VEC, BS), F32),
-            pltpu.VMEM((G, PAIR_ROWS, BS), F32),
-            pltpu.VMEM((VEC, VEC), F32),
+            pltpu.VMEM((2 * chunk, 2 * BS), BF16),
+            pltpu.VMEM((2 * chunk, 2 * chunk), F32),
+            pltpu.VMEM((nb, 1, BS), F32),
+            pltpu.VMEM((wide, 1, BS), F32),
+            pltpu.VMEM((VEC, VEC, wide), F32),
             pltpu.VMEM((VEC * VEC, VEC, BS), F32),
             pltpu.VMEM((VEC * VEC, VEC, BS), F32),
             dma((5,)),
@@ -436,14 +493,15 @@
             dma((DEG, G, 2)),
             dma((1,)),
             dma((1,)),
-            dma((G,)),
-            dma((G,)),
+            dma((1,)),
+            dma((1,)),
+            pltpu.SemaphoreType.REGULAR((max(1, len(reach_steps(wide))),)),
         ],
         compiler_params=pltpu.CompilerParams(
-            collective_id=0, has_side_effects=True, vmem_limit_bytes=40 * 1024 * 1024
+            collective_id=0, has_side_effects=True, vmem_limit_bytes=60 * 1024 * 1024
         ),
         cost_estimate=pl.CostEstimate(flops=3 * 10**9, bytes_accessed=2 * 1024 * 1024, transcendentals=0),
-    )(slab.reshape(2 * states, BS), hblocks.reshape(2, K, BS, BS), codes, rotation)
+    )(slab.reshape(2 * states, BS), hblocks.reshape(2, K, BS, BS), blist, jnp.transpose(rotation, (1, 2, 0)))
 
 
 def solution(mesh):

time: 84.2 us -> 75.8 us (0.900)
  Pallas kernels: 79.4 us -> 73.8 us
  local copies, waits for them, and re-layouts: 4.51 us -> 1.87 us
    pallas_call x1, Pallas kernels: 79.4 us -> 73.8 us  [body(): pl.pallas_call(functools.partial(kernel, wide, nodes), out_shape=jax.Shap...]
    unnamed x8 -> x1, local copies, waits for them, and re-layouts: 4.51 us -> 1.87 us
where the time goes in v2:
time: 75.8 us; the launch traced here: 75.7 us
  Pallas kernels  73.8 us (97%)
  local copies, waits for them, and re-layouts  1.87 us (2%)
    pallas_call x1, Pallas kernels, body(): pl.pallas_call(functools.partial(kernel, wide, nodes), out_shape=jax.Shap...  73.8 us
    unnamed x1, local copies, waits for them, and re-layouts  1.87 us

profile of v2, /device:TPU:1, one launch (start us, length us, event | category | flops | bytes accessed | tf_op | source)
XLA Modules:
  0.0 75.7 jit_solution(2824895432734241577)
XLA Ops:
  0.0 73.8 %shard_map.46 = f32[8,1,128,128]{3,2,1,0:T(8,128)} custom-call(f32[1024,128]{1,0:T(8,128)} %bitcast.4, f32[2,5,128,128]{3,2,1,0:T(8,128)} %bitcast.3, s32[1,2,5]{2,1,0:T(2,128)} %blist.1, f32[8,8,64]{2,1,0:T(8,128)} %bitcast.5), custom_call_target="tpu_custom_call" | custom-call | flops 3000000000 | bytes 2097152 | tf_op jit(solution)/shard_map/pallas_call | solution.py:461
  73.8 1.9 %copy.6 = f32[8,1,128,128]{3,2,1,0:T(8,128)} copy(f32[8,1,128,128]{3,2,1,0:T(8,128)} %shard_map.46) | data formatting | bytes 1048576

commit v3 on v2

--- a/solution.py
+++ b/solution.py
@@ -113,20 +113,20 @@
     own_rot.start()
 
     zero = jnp.zeros((2 * chunk, BS), BF16)
-    for parity in range(2):
+    for n in range(DEG):
         for col in range(4):
-            xs[parity, col] = zero
-            xs[parity, 20 + col] = zero
+            xs[n, col] = zero
+            xs[n, 20 + col] = zero
 
         @pl.when(jnp.logical_not(has_left))
         def _():
             for r in range(G):
-                xs[parity, (r + 1) * 4] = zero
+                xs[n, (r + 1) * 4] = zero
 
         @pl.when(jnp.logical_not(has_right))
         def _():
             for r in range(G):
-                xs[parity, (r + 1) * 4 + 3] = zero
+                xs[n, (r + 1) * 4 + 3] = zero
 
     pl.semaphore_wait(barrier, G + 1)
 
@@ -178,10 +178,10 @@
                 hs[r, q, 0:BS, k * BS : (k + 1) * BS] = high
                 hs[r, q, BS : 2 * BS, k * BS : (k + 1) * BS] = low
 
-    def store_split(parity, position, value):
+    def store_split(n, position, value):
         high, low = split(value)
-        xs[parity, position, 0:chunk] = high
-        xs[parity, position, chunk : 2 * chunk] = low
+        xs[n, position, 0:chunk] = high
+        xs[n, position, chunk : 2 * chunk] = low
 
     def halo_copy(n, r, side):
         to = w - 1 if side == 0 else w + 1
@@ -202,24 +202,19 @@
         def _():
             halo_copy(n, r, 1).start()
 
-    def take_halos(n):
-        parity = n % 2
-
-        @pl.loop(0, G)
-        def _(r):
-            @pl.when(has_left)
-            def _():
-                halo_copy(n, r, 1).wait_recv()
-                store_split(parity, (r + 1) * 4, halo[n, r, 0])
-
-            @pl.when(has_right)
-            def _():
-                halo_copy(n, r, 0).wait_recv()
-                store_split(parity, (r + 1) * 4 + 3, halo[n, r, 1])
+    def take_halos(n, r):
+        @pl.when(has_left)
+        def _():
+            halo_copy(n, r, 1).wait_recv()
+            store_split(n, (r + 1) * 4, halo[n, r, 0])
+
+        @pl.when(has_right)
+        def _():
+            halo_copy(n, r, 0).wait_recv()
+            store_split(n, (r + 1) * 4 + 3, halo[n, r, 1])
 
     def product(n, r, q):
-        parity = n % 2
-        picked = [xs[parity, r * 4 + position_sm[r, q * 8 + k]] for k in range(K)]
+        picked = [xs[n, r * 4 + position_sm[r, q * 8 + k]] for k in range(K)]
         both = jnp.concatenate(picked, axis=1)
         p = lax.dot_general(both, hs[r, q], (((1,), (1,)), ((), ())), preferred_element_type=F32)
         small = p[:chunk, BS:] + p[chunk:, :BS] + p[chunk:, BS:]
@@ -232,7 +227,7 @@
                 value = 2.0 * value - fields[n - 1, r, q]
             if n + 1 < DEG:
                 fields[n + 1, r, q] = value
-                store_split((n + 1) % 2, (r + 1) * 4 + 1 + q, value)
+                store_split(n + 1, (r + 1) * 4 + 1 + q, value)
             else:
                 fin[r, :, q * VEC : (q + 1) * VEC, :] = value.reshape(nb, VEC, BS)
                 high, low = split(value)
@@ -287,7 +282,11 @@
             greeted(waiting.pop(0))
 
     next_round()
-    take_halos(0)
+
+    @pl.loop(0, G)
+    def _(r):
+        take_halos(0, r)
+
     apply_row(0, g)
     next_round()
     h_wait(3, 0)
@@ -304,49 +303,80 @@
     apply_row(0, row_at(1))
     while waiting:
         next_round()
+    for d in (0, 3, 1):
+        take_halos(1, row_at(d))
+    apply_row(1, g)
     h_wait(2, 0)
     h_wait(2, 1)
     split_h(row_at(2))
     apply_row(0, row_at(2))
 
-    for n in range(1, DEG - 1):
-        take_halos(n)
+    take_halos(1, row_at(2))
+
+    @pl.loop(0, G)
+    def _(r):
+        @pl.when(r != g)
+        def _():
+            apply_row(1, r)
+
+    def wave(n, then):
+        take_halos(n, 0)
 
         @pl.loop(0, G)
         def _(r):
+            @pl.when(r < G - 1)
+            def _():
+                take_halos(n, r + 1)
+
             apply_row(n, r)
-
-    take_halos(DEG - 1)
-
-    def to_owners(r, block_copy, local_copy):
-        @pl.loop(0, nb)
-        def _(i):
-            b = lax.rem(i + w, nb)
-            to = g * nb + b
-            own = jnp.logical_and(to == w, r == g)
-
-            @pl.when(jnp.logical_not(own))
-            def _():
-                block_copy(b, (to, r)).start()
-
-            @pl.when(own)
-            def _():
-                local_copy(b).start()
-
-    gram_all[...] = jnp.zeros_like(gram_all)
-
-    @pl.loop(0, G)
-    def _(d):
-        r = row_at(d)
-        apply_row(DEG - 1, r)
+            then(r)
+
+    for n in range(2, DEG - 1):
+        wave(n, lambda r: None)
+
+    cores = min(2, nb)
+    ring = nb // cores
+    offsets = sorted(range(ring), key=lambda d: -min(d, ring - d))
+    far = [d for d in offsets if min(d, ring - d) > 1]
+    near = [d for d in offsets if min(d, ring - d) <= 1]
+
+    def to_owners(r, distances, block_copy, local_copy):
+        place = lax.rem(w, nb)
+        for d in distances:
+            for other in reversed(range(cores)):
+                b = lax.rem(place // cores + d, ring) * cores + lax.rem(place + other, cores)
+                to = g * nb + b
+                if d == 0 and other == 0:
+                    own = jnp.logical_and(to == w, r == g)
+
+                    @pl.when(jnp.logical_not(own))
+                    def _():
+                        block_copy(b, (to, r)).start()
+
+                    @pl.when(own)
+                    def _():
+                        local_copy(b).start()
+
+                else:
+                    block_copy(b, (to, r)).start()
+
+    def send_blocks(r, distances):
         slot = recv.at[pl.ds(w * 2 * VEC, 2 * VEC)]
         to_owners(
             r,
+            distances,
             lambda b, to: remote(fin.at[r, b], slot, fin_send.at[0], fin_recv.at[0], to),
             lambda b: pltpu.make_async_copy(fin.at[r, b], slot, fin_recv.at[0]),
         )
+
+    gram_all[...] = jnp.zeros_like(gram_all)
+
+    def last(r):
+        send_blocks(r, far)
         both = both_last[...]
         gram_all[...] += lax.dot_general(both, both, (((1,), (1,)), ((), ())), preferred_element_type=F32)
+
+    wave(DEG - 1, last)
 
     states_gram = (gram_all[:chunk, chunk:] + gram_all[chunk:, :chunk] + gram_all[chunk:, chunk:]) + gram_all[:chunk, :chunk]
     row_id = lax.broadcasted_iota(jnp.int32, (chunk, chunk), 0)
@@ -366,9 +396,14 @@
         r = row_at(d)
         to_owners(
             r,
+            offsets,
             lambda b, to: remote(gram_out.at[b], gram_in.at[w], gram_send.at[0], gram_recv.at[0], to),
             lambda b: pltpu.make_async_copy(gram_out.at[b], gram_in.at[w], gram_recv.at[0]),
         )
+
+    @pl.loop(0, G)
+    def _(r):
+        send_blocks(r, near)
 
     arrived(gram_in, gram_recv.at[0])
     whole = jnp.sum(gram_in[...], axis=0) * (1.0 / nodes)
@@ -457,7 +492,9 @@
     nb = wide // G
     nodes = G * 2 * wide * BS
     dma = pltpu.SemaphoreType.DMA
-    any_space = pl.BlockSpec(memory_space=pl.ANY)
+    any_space = pl.BlockSpec(memory_space=pltpu.HBM)
+    operands = (slab.reshape(2 * states, BS), hblocks.reshape(2, K, BS, BS), blist, jnp.transpose(rotation, (1, 2, 0)))
+    operands = [pltpu.with_memory_space_constraint(value, pltpu.HBM) for value in operands]
     return pl.pallas_call(
         functools.partial(kernel, wide, nodes),
         out_shape=jax.ShapeDtypeStruct((VEC, 1, 2 * wide, BS), F32),
@@ -472,7 +509,7 @@
             pltpu.VMEM((G, 2, 2 * BS, K * BS), BF16),
             pltpu.VMEM((DEG, G, 2, chunk, BS), F32),
             pltpu.VMEM((DEG, G, 2, chunk, BS), F32),
-            pltpu.VMEM((2, 24, 2 * chunk, BS), BF16),
+            pltpu.VMEM((DEG, 24, 2 * chunk, BS), BF16),
             pltpu.VMEM((G, nb, 2 * VEC, BS), F32),
             pltpu.VMEM((wide * 2 * VEC, BS), F32),
             pltpu.VMEM((2 * chunk, 2 * BS), BF16),
@@ -498,10 +535,10 @@
             pltpu.SemaphoreType.REGULAR((max(1, len(reach_steps(wide))),)),
         ],
         compiler_params=pltpu.CompilerParams(
-            collective_id=0, has_side_effects=True, vmem_limit_bytes=60 * 1024 * 1024
+            collective_id=0, has_side_effects=True, vmem_limit_bytes=40 * 1024 * 1024
         ),
         cost_estimate=pl.CostEstimate(flops=3 * 10**9, bytes_accessed=2 * 1024 * 1024, transcendentals=0),
-    )(slab.reshape(2 * states, BS), hblocks.reshape(2, K, BS, BS), blist, jnp.transpose(rotation, (1, 2, 0)))
+    )(*operands)
 
 
 def solution(mesh):

time: 75.8 us -> 71.2 us (0.939)
  Pallas kernels: 73.8 us -> 70.3 us
  local copies, waits for them, and re-layouts: 1.87 us -> 0.8 us
    pallas_call x1, Pallas kernels: 73.8 us -> 70.3 us  [body(): pl.pallas_call(functools.partial(kernel, wide, nodes), out_shape=jax.Shap...]
    unnamed x1, local copies, waits for them, and re-layouts: 1.87 us -> 0.8 us
where the time goes in v3:
time: 71.2 us
  Pallas kernels  70.3 us (99%)
  local copies, waits for them, and re-layouts  0.8 us (1%)
    pallas_call x1, Pallas kernels, body(): pl.pallas_call(functools.partial(kernel, wide, nodes), out_shape=jax.Shap...  70.3 us

profile of v3, /device:TPU:1, one launch (start us, length us, event | category | flops | bytes accessed | tf_op | source)
XLA Modules:
  0.0 71.2 jit_solution(15898143048340915490)
XLA Ops:
  0.0 70.3 %shard_map.46 = f32[8,1,128,128]{3,2,1,0:T(8,128)S(1)} custom-call(f32[1024,128]{1,0:T(8,128)} %bitcast.4, f32[2,5,128,128]{3,2,1,0:T(8,128)} %bitcast.3, s32[1,2,5]{2,1,0:T(2,128)} %blist.1, f32[8,8,64]{2,1,0:T(8,128)} %bitcast.5), custom_call_target="tpu_custom_call" | custom-call | flops 3000000000 | bytes 2097152 | tf_op jit(solution)/shard_map/pallas_call | solution.py:498
  70.4 0.8 %copy.6 = f32[8,1,128,128]{3,2,1,0:T(8,128)} copy(f32[8,1,128,128]{3,2,1,0:T(8,128)S(1)} %shard_map.46) | data formatting | bytes 1048576

commit v4 on v3

--- a/solution.py
+++ b/solution.py
@@ -81,6 +81,8 @@
     is_own = source == g
     has_left = w > 0
     has_right = w < wide - 1
+    first = lax.rem(w, 2)
+    other = 1 - first
 
     def remote(src, dst, send_sem, recv_sem, to):
         return pltpu.make_async_remote_copy(
@@ -155,11 +157,11 @@
             hblocks.at[half], h_in.at[g, half], h_send.at[half, d // 2], h_recv.at[g, half], (w, row_at(d))
         )
 
-    def h_forward(half, d):
+    def h_forward(half):
+        d = 1 + 2 * half
         origin = row_at(G - d)
-        return remote(
-            h_in.at[origin, half], h_in.at[origin, half], h_send.at[half, 2], h_recv.at[origin, half], (w, row_at(d))
-        )
+        block = h_in.at[origin, half]
+        return remote(block, block, h_send.at[half, 2], h_recv.at[origin, half], (w, row_at(d)))
 
     for d in (1, 3, 2):
         slab_copy(d).start()
@@ -170,13 +172,15 @@
     h_copy(1, 1).start()
     h_copy(0, 3).start()
 
+    def split_column(r, q):
+        for k in range(K):
+            high, low = split(h_in[r, q, k])
+            hs[r, q, 0:BS, k * BS : (k + 1) * BS] = high
+            hs[r, q, BS : 2 * BS, k * BS : (k + 1) * BS] = low
+
     def split_h(r):
-        @pl.loop(0, 2)
-        def _(q):
-            for k in range(K):
-                high, low = split(h_in[r, q, k])
-                hs[r, q, 0:BS, k * BS : (k + 1) * BS] = high
-                hs[r, q, BS : 2 * BS, k * BS : (k + 1) * BS] = low
+        for q in range(2):
+            split_column(r, q)
 
     def store_split(n, position, value):
         high, low = split(value)
@@ -184,23 +188,20 @@
         xs[n, position, chunk : 2 * chunk] = low
 
     def halo_copy(n, r, side):
-        to = w - 1 if side == 0 else w + 1
         return remote(
             fields.at[n, r, side],
             halo.at[n, r, 1 - side],
             halo_send.at[n, r, side],
             halo_recv.at[n, r, 1 - side],
-            (to, g),
+            (w - 1 + 2 * side, g),
         )
 
-    def send_halos(n, r):
-        @pl.when(has_left)
+    def send_halo(n, r, side):
+        to = w - 1 + 2 * side
+
+        @pl.when(jnp.logical_and(to >= 0, to < wide))
         def _():
-            halo_copy(n, r, 0).start()
-
-        @pl.when(has_right)
-        def _():
-            halo_copy(n, r, 1).start()
+            halo_copy(n, r, side).start()
 
     def take_halos(n, r):
         @pl.when(has_left)
@@ -220,21 +221,23 @@
         small = p[:chunk, BS:] + p[chunk:, :BS] + p[chunk:, BS:]
         return p[:chunk, :BS] + small
 
-    def apply_row(n, r):
-        for q in range(2):
+    def apply(n, blocks):
+        values = []
+        for r, q in blocks:
             value = product(n, r, q)
-            if n > 0:
-                value = 2.0 * value - fields[n - 1, r, q]
+            values.append(2.0 * value - fields[n - 1, r, q] if n > 0 else value)
+        for (r, q), value in zip(blocks, values):
             if n + 1 < DEG:
                 fields[n + 1, r, q] = value
                 store_split(n + 1, (r + 1) * 4 + 1 + q, value)
             else:
                 fin[r, :, q * VEC : (q + 1) * VEC, :] = value.reshape(nb, VEC, BS)
                 high, low = split(value)
-                both_last[0:chunk, q * BS : (q + 1) * BS] = high
-                both_last[chunk : 2 * chunk, q * BS : (q + 1) * BS] = low
+                both_last[r, 0:chunk, q * BS : (q + 1) * BS] = high
+                both_last[r, chunk : 2 * chunk, q * BS : (q + 1) * BS] = low
         if n + 1 < DEG:
-            send_halos(n + 1, r)
+            for r, q in blocks:
+                send_halo(n + 1, r, q)
 
     own_h.wait()
     split_h(g)
@@ -250,7 +253,8 @@
             value = slab_in[r, pl.ds(q, chunk, stride=2), :]
             fields[0, r, q] = value
             store_split(0, (r + 1) * 4 + 1 + q, value)
-        send_halos(0, r)
+        send_halo(0, r, first)
+        send_halo(0, r, other)
 
     own_slab.wait()
     start_row(g)
@@ -287,52 +291,41 @@
     def _(r):
         take_halos(0, r)
 
-    apply_row(0, g)
+    apply(0, [(g, first), (g, other)])
     next_round()
-    h_wait(3, 0)
-    h_forward(0, 1).start()
-    h_wait(1, 1)
-    h_forward(1, 3).start()
+
+    h_wait(G - 1 - 2 * first, first)
+    h_forward(first).start()
+    h_wait(G - 1 - 2 * other, other)
     next_round()
     h_wait(3, 1)
+    h_forward(other).start()
     split_h(row_at(3))
-    apply_row(0, row_at(3))
+    apply(0, [(row_at(3), first), (row_at(3), other)])
     next_round()
     h_wait(1, 0)
     split_h(row_at(1))
-    apply_row(0, row_at(1))
+    apply(0, [(row_at(1), first), (row_at(1), other)])
     while waiting:
         next_round()
     for d in (0, 3, 1):
         take_halos(1, row_at(d))
-    apply_row(1, g)
-    h_wait(2, 0)
-    h_wait(2, 1)
-    split_h(row_at(2))
-    apply_row(0, row_at(2))
+    apply(1, [(g, first), (g, other)])
+    for q in (first, other):
+        h_wait(2, q)
+        split_column(row_at(2), q)
+        apply(0, [(row_at(2), q)])
 
     take_halos(1, row_at(2))
-
-    @pl.loop(0, G)
-    def _(r):
-        @pl.when(r != g)
-        def _():
-            apply_row(1, r)
-
-    def wave(n, then):
-        take_halos(n, 0)
-
-        @pl.loop(0, G)
-        def _(r):
-            @pl.when(r < G - 1)
-            def _():
-                take_halos(n, r + 1)
-
-            apply_row(n, r)
-            then(r)
-
-    for n in range(2, DEG - 1):
-        wave(n, lambda r: None)
+    for q in (first, other):
+        apply(1, [(row_at(d), q) for d in (3, 1, 2)])
+
+    for r in range(3):
+        take_halos(2, r)
+    apply(2, [(0, first), (1, first)])
+    take_halos(2, 3)
+    apply(2, [(2, first), (3, first)])
+    apply(2, [(r, other) for r in range(G)])
 
     cores = min(2, nb)
     ring = nb // cores
@@ -371,12 +364,20 @@
 
     gram_all[...] = jnp.zeros_like(gram_all)
 
-    def last(r):
-        send_blocks(r, far)
-        both = both_last[...]
-        gram_all[...] += lax.dot_general(both, both, (((1,), (1,)), ((), ())), preferred_element_type=F32)
-
-    wave(DEG - 1, last)
+    def last(rows):
+        for r in rows:
+            send_blocks(r, far)
+        for r in rows:
+            both = both_last[r]
+            gram_all[...] += lax.dot_general(both, both, (((1,), (1,)), ((), ())), preferred_element_type=F32)
+
+    for r in range(3):
+        take_halos(DEG - 1, r)
+    apply(DEG - 1, [(r, q) for r in (0, 1) for q in range(2)])
+    last((0, 1))
+    take_halos(DEG - 1, 3)
+    apply(DEG - 1, [(r, q) for r in (2, 3) for q in range(2)])
+    last((2, 3))
 
     states_gram = (gram_all[:chunk, chunk:] + gram_all[chunk:, :chunk] + gram_all[chunk:, chunk:]) + gram_all[:chunk, :chunk]
     row_id = lax.broadcasted_iota(jnp.int32, (chunk, chunk), 0)
@@ -457,8 +458,8 @@
     for half in range(2):
         h_copy(half, 1).wait_send()
         h_copy(half, 3).wait_send()
-    h_forward(0, 1).wait_send()
-    h_forward(1, 3).wait_send()
+    h_forward(first).wait_send()
+    h_forward(other).wait_send()
 
     @pl.loop(0, DEG)
     def _(n):
@@ -512,7 +513,7 @@
             pltpu.VMEM((DEG, 24, 2 * chunk, BS), BF16),
             pltpu.VMEM((G, nb, 2 * VEC, BS), F32),
             pltpu.VMEM((wide * 2 * VEC, BS), F32),
-            pltpu.VMEM((2 * chunk, 2 * BS), BF16),
+            pltpu.VMEM((G, 2 * chunk, 2 * BS), BF16),
             pltpu.VMEM((2 * chunk, 2 * chunk), F32),
             pltpu.VMEM((nb, 1, BS), F32),
             pltpu.VMEM((wide, 1, BS), F32),

time: 71.2 us -> 69.6 us (0.978)
  Pallas kernels: 70.3 us -> 68.8 us
    pallas_call x1, Pallas kernels: 70.3 us -> 68.8 us  [body(): pl.pallas_call(functools.partial(kernel, wide, nodes), out_shape=jax.Shap...]
where the time goes in v4:
time: 69.6 us
  Pallas kernels  68.8 us (99%)
  local copies, waits for them, and re-layouts  0.8 us (1%)
    pallas_call x1, Pallas kernels, body(): pl.pallas_call(functools.partial(kernel, wide, nodes), out_shape=jax.Shap...  68.8 us

profile of v4, /device:TPU:1, one launch (start us, length us, event | category | flops | bytes accessed | tf_op | source)
XLA Modules:
  0.0 69.6 jit_solution(2105945228188804879)
XLA Ops:
  0.0 68.8 %shard_map.46 = f32[8,1,128,128]{3,2,1,0:T(8,128)S(1)} custom-call(f32[1024,128]{1,0:T(8,128)} %bitcast.4, f32[2,5,128,128]{3,2,1,0:T(8,128)} %bitcast.3, s32[1,2,5]{2,1,0:T(2,128)} %blist.1, f32[8,8,64]{2,1,0:T(8,128)} %bitcast.5), custom_call_target="tpu_custom_call" | custom-call | flops 3000000000 | bytes 2097152 | tf_op jit(solution)/shard_map/pallas_call | solution.py:499
  68.8 0.8 %copy.6 = f32[8,1,128,128]{3,2,1,0:T(8,128)} copy(f32[8,1,128,128]{3,2,1,0:T(8,128)S(1)} %shard_map.46) | data formatting | bytes 1048576

commit v5 on v4

--- a/solution.py
+++ b/solution.py
@@ -167,10 +167,10 @@
         slab_copy(d).start()
     for d in (1, 3, 2):
         codes_copy(d).start()
-    h_copy(0, 1).start()
-    h_copy(1, 3).start()
-    h_copy(1, 1).start()
-    h_copy(0, 3).start()
+    h_copy(first, 1 + 2 * first).start()
+    h_copy(first, 3 - 2 * first).start()
+    h_copy(other, 1 + 2 * other).start()
+    h_copy(other, 3 - 2 * other).start()
 
     def split_column(r, q):
         for k in range(K):
@@ -294,27 +294,27 @@
     apply(0, [(g, first), (g, other)])
     next_round()
 
-    h_wait(G - 1 - 2 * first, first)
-    h_forward(first).start()
-    h_wait(G - 1 - 2 * other, other)
+    def take_h(d, q, forward):
+        h_wait(d, q)
+        if forward:
+            h_forward(q).start()
+        split_column(row_at(d), q)
+        apply(0, [(row_at(d), q)])
+
+    take_h(G - 1 - 2 * first, first, True)
     next_round()
-    h_wait(3, 1)
-    h_forward(other).start()
-    split_h(row_at(3))
-    apply(0, [(row_at(3), first), (row_at(3), other)])
+    take_h(1 + 2 * first, first, False)
     next_round()
-    h_wait(1, 0)
-    split_h(row_at(1))
-    apply(0, [(row_at(1), first), (row_at(1), other)])
+    take_h(1 + 2 * first, other, True)
+    next_round()
+    take_h(G - 1 - 2 * first, other, False)
     while waiting:
         next_round()
+    take_h(2, first, False)
     for d in (0, 3, 1):
         take_halos(1, row_at(d))
     apply(1, [(g, first), (g, other)])
-    for q in (first, other):
-        h_wait(2, q)
-        split_column(row_at(2), q)
-        apply(0, [(row_at(2), q)])
+    take_h(2, other, False)
 
     take_halos(1, row_at(2))
     for q in (first, other):

time: 69.6 us -> 69 us (level)
  Pallas kernels: 68.8 us -> 68.1 us
where the time goes in v5:
time: 69 us; the launch traced here: 68.9 us
  Pallas kernels  68.1 us (99%)
  local copies, waits for them, and re-layouts  0.8 us (1%)
    pallas_call x1, Pallas kernels, body(): pl.pallas_call(functools.partial(kernel, wide, nodes), out_shape=jax.Shap...  68.1 us

profile of v5, /device:TPU:1, one launch (start us, length us, event | category | flops | bytes accessed | tf_op | source)
XLA Modules:
  0.0 68.9 jit_solution(16121590752594532336)
XLA Ops:
  0.0 68.1 %shard_map.46 = f32[8,1,128,128]{3,2,1,0:T(8,128)S(1)} custom-call(f32[1024,128]{1,0:T(8,128)} %bitcast.4, f32[2,5,128,128]{3,2,1,0:T(8,128)} %bitcast.3, s32[1,2,5]{2,1,0:T(2,128)} %blist.1, f32[8,8,64]{2,1,0:T(8,128)} %bitcast.5), custom_call_target="tpu_custom_call" | custom-call | flops 3000000000 | bytes 2097152 | tf_op jit(solution)/shard_map/pallas_call | solution.py:499
  68.1 0.8 %copy.6 = f32[8,1,128,128]{3,2,1,0:T(8,128)} copy(f32[8,1,128,128]{3,2,1,0:T(8,128)S(1)} %shard_map.46) | data formatting | bytes 1048576

commit v6 on v5

--- a/solution.py
+++ b/solution.py
@@ -174,9 +174,9 @@
 
     def split_column(r, q):
         for k in range(K):
-            high, low = split(h_in[r, q, k])
-            hs[r, q, 0:BS, k * BS : (k + 1) * BS] = high
-            hs[r, q, BS : 2 * BS, k * BS : (k + 1) * BS] = low
+            high, low = split(h_in[r, q, k].T)
+            hs[r, q, k * BS : (k + 1) * BS, 0:BS] = high
+            hs[r, q, k * BS : (k + 1) * BS, BS : 2 * BS] = low
 
     def split_h(r):
         for q in range(2):
@@ -217,7 +217,7 @@
     def product(n, r, q):
         picked = [xs[n, r * 4 + position_sm[r, q * 8 + k]] for k in range(K)]
         both = jnp.concatenate(picked, axis=1)
-        p = lax.dot_general(both, hs[r, q], (((1,), (1,)), ((), ())), preferred_element_type=F32)
+        p = jnp.dot(both, hs[r, q], preferred_element_type=F32)
         small = p[:chunk, BS:] + p[chunk:, :BS] + p[chunk:, BS:]
         return p[:chunk, :BS] + small
 
@@ -287,6 +287,9 @@
 
     next_round()
 
+    h_wait(G - 1 - 2 * first, first)
+    h_forward(first).start()
+
     @pl.loop(0, G)
     def _(r):
         take_halos(0, r)
@@ -301,7 +304,8 @@
         split_column(row_at(d), q)
         apply(0, [(row_at(d), q)])
 
-    take_h(G - 1 - 2 * first, first, True)
+    split_column(row_at(G - 1 - 2 * first), first)
+    apply(0, [(row_at(G - 1 - 2 * first), first)])
     next_round()
     take_h(1 + 2 * first, first, False)
     next_round()
@@ -507,7 +511,7 @@
             pltpu.VMEM((G, 2, K), jnp.int32),
             pltpu.SMEM((G, 2, K), jnp.int32),
             pltpu.SMEM((G, 16), jnp.int32),
-            pltpu.VMEM((G, 2, 2 * BS, K * BS), BF16),
+            pltpu.VMEM((G, 2, K * BS, 2 * BS), BF16),
             pltpu.VMEM((DEG, G, 2, chunk, BS), F32),
             pltpu.VMEM((DEG, G, 2, chunk, BS), F32),
             pltpu.VMEM((DEG, 24, 2 * chunk, BS), BF16),

time: 69 us -> 68.8 us (level)
  no operation moved by 1% of the time
where the time goes in v6:
time: 68.8 us; the launch traced here: 68.6 us
  Pallas kernels  67.8 us (99%)
  local copies, waits for them, and re-layouts  0.8 us (1%)
    pallas_call x1, Pallas kernels, body(): pl.pallas_call(functools.partial(kernel, wide, nodes), out_shape=jax.Shap...  67.8 us

profile of v6, /device:TPU:1, one launch (start us, length us, event | category | flops | bytes accessed | tf_op | source)
XLA Modules:
  0.0 68.6 jit_solution(11017832543419467767)
XLA Ops:
  0.0 67.8 %shard_map.46 = f32[8,1,128,128]{3,2,1,0:T(8,128)S(1)} custom-call(f32[1024,128]{1,0:T(8,128)} %bitcast.4, f32[2,5,128,128]{3,2,1,0:T(8,128)} %bitcast.3, s32[1,2,5]{2,1,0:T(2,128)} %blist.1, f32[8,8,64]{2,1,0:T(8,128)} %bitcast.5), custom_call_target="tpu_custom_call" | custom-call | flops 3000000000 | bytes 2097152 | tf_op jit(solution)/shard_map/pallas_call | solution.py:503
  67.8 0.8 %copy.6 = f32[8,1,128,128]{3,2,1,0:T(8,128)} copy(f32[8,1,128,128]{3,2,1,0:T(8,128)S(1)} %shard_map.46) | data formatting | bytes 1048576

commit v7 on v6

--- a/solution.py
+++ b/solution.py
@@ -326,7 +326,8 @@
 
     for r in range(3):
         take_halos(2, r)
-    apply(2, [(0, first), (1, first)])
+    apply(2, [(0, first)])
+    apply(2, [(1, first)])
     take_halos(2, 3)
     apply(2, [(2, first), (3, first)])
     apply(2, [(r, other) for r in range(G)])
@@ -377,8 +378,9 @@
 
     for r in range(3):
         take_halos(DEG - 1, r)
-    apply(DEG - 1, [(r, q) for r in (0, 1) for q in range(2)])
-    last((0, 1))
+    for r in (0, 1):
+        apply(DEG - 1, [(r, 0), (r, 1)])
+        last((r,))
     take_halos(DEG - 1, 3)
     apply(DEG - 1, [(r, q) for r in (2, 3) for q in range(2)])
     last((2, 3))

time: 68.8 us -> 68.8 us (level)
  no operation moved by 1% of the time
where the time goes in v7:
time: 68.8 us; the launch traced here: 68.3 us
  Pallas kernels  67.5 us (98%)
  local copies, waits for them, and re-layouts  0.8 us (1%)
    pallas_call x1, Pallas kernels, body(): pl.pallas_call(functools.partial(kernel, wide, nodes), out_shape=jax.Shap...  67.5 us

profile of v7, /device:TPU:1, one launch (start us, length us, event | category | flops | bytes accessed | tf_op | source)
XLA Modules:
  0.0 68.3 jit_solution(7361131124804763131)
XLA Ops:
  0.0 67.5 %shard_map.46 = f32[8,1,128,128]{3,2,1,0:T(8,128)S(1)} custom-call(f32[1024,128]{1,0:T(8,128)} %bitcast.4, f32[2,5,128,128]{3,2,1,0:T(8,128)} %bitcast.3, s32[1,2,5]{2,1,0:T(2,128)} %blist.1, f32[8,8,64]{2,1,0:T(8,128)} %bitcast.5), custom_call_target="tpu_custom_call" | custom-call | flops 3000000000 | bytes 2097152 | tf_op jit(solution)/shard_map/pallas_call | solution.py:505
  67.5 0.8 %copy.6 = f32[8,1,128,128]{3,2,1,0:T(8,128)} copy(f32[8,1,128,128]{3,2,1,0:T(8,128)S(1)} %shard_map.46) | data formatting | bytes 1048576
